TPU v7x, 256 devices: a whole 4x4x8 slice. The times are simulated.
256 devices in a mesh: dp: 32 (over x_hi, z, core), tensor: 8 (over x_lo, y).
Axes of the slice: x: 4 (x_hi: 2, x_lo: 2; x = x_hi * 2 + x_lo), y: 4, z: 8, core: 2. Of those that a mesh axis runs over, the one named last changes fastest.
Arguments:
- acts: bfloat16 [65536, 8192], P('dp', 'tensor'), may hold values from -6 to 6
- cotangent: bfloat16 [65536, 8192], P(('dp', 'tensor')), may hold values from -6 to 6
- down_weight: bfloat16 [8192, 16], P('tensor'), may hold values from -0.0625 to 0.0625
- project: bfloat16 [8192, 512], P('tensor'), may hold values from -0.0625 to 0.0625
- queries: bfloat16 [4096, 8192], P('dp', 'tensor'), may hold values from -6 to 6
Outputs:
- scores: float32 [4096, 64], P('dp')
All inputs are finite; a program needn't handle non-finite values.
Results may differ from a plain program's by a relative error of at most 0.0041.
Values may be sent and summed in bfloat16 or wider, within the bound.
A program may use at most 64 MiB of HBM per device.

v0:
```python
import jax
import jax.numpy as jnp
from jax import lax
from jax.sharding import PartitionSpec as P

ADAPTER_RANK = 16
PK = 512
LENGTH = 1024
SEQ_DEV = 2


def solve_factor(factor, rhs):
    middle = lax.linalg.triangular_solve(factor, rhs, left_side=True, lower=True, transpose_a=False)
    return lax.linalg.triangular_solve(factor, middle, left_side=True, lower=True, transpose_a=True)


def shards(acts, cotangent, down_weight, project, queries):
    partial_input_rows = jnp.dot(acts, down_weight, preferred_element_type=jnp.float32)
    summed = lax.psum(partial_input_rows, "tensor")
    input_rows = summed.astype(jnp.bfloat16).reshape(SEQ_DEV, LENGTH, ADAPTER_RANK)
    columns = lax.all_to_all(cotangent, "tensor", split_axis=1, concat_axis=0, tiled=True)
    columns = columns.reshape(SEQ_DEV, LENGTH, columns.shape[1])
    grads = jnp.einsum("etr,etd->erd", input_rows, columns, preferred_element_type=jnp.float32)
    grads = grads.astype(jnp.bfloat16)
    partial_proj = jnp.einsum("erd,dk->erk", grads, project, preferred_element_type=jnp.float32)
    partial_proj = partial_proj.reshape(SEQ_DEV, ADAPTER_RANK * PK)
    reduced = lax.psum_scatter(partial_proj, "tensor", scatter_dimension=1, tiled=True)
    table = lax.all_gather(reduced, "dp", axis=0, tiled=True)
    kernel_part = jnp.dot(table, table.T, precision=lax.Precision.HIGHEST)
    cross_part = jnp.dot(queries.astype(jnp.float32), table.T, precision=lax.Precision.HIGHEST)
    kernel, cross = lax.psum((kernel_part, cross_part), "tensor")
    examples = kernel.shape[0]
    shift = 0.5 * jnp.trace(kernel) / examples
    damped_system = kernel + shift * jnp.eye(examples, dtype=jnp.float32)
    factor = jnp.linalg.cholesky(damped_system)
    solved = solve_factor(factor, cross.T)
    return examples * solved.T


def solution(mesh):
    placed = (
        P("dp", "tensor"),
        P(("dp", "tensor"), None),
        P("tensor", None),
        P("tensor", None),
        P("dp", "tensor"),
    )
    return jax.shard_map(
        shards, mesh=mesh, in_specs=placed, out_specs=P("dp", None), check_vma=False
    )
```

profile of v0, /device:TPU:2, one launch (start us, length us, event | category | flops | bytes accessed | tf_op | source)
XLA Modules:
  0.0 259.8 jit_solution(16744589437896677063)
XLA Ops:
  6.5 0.0 copy-start
  6.5 6.5 %copy.12 = bf16[256,8192]{0,1:T(8,128)(2,1)} copy(bf16[256,8192]{1,0:T(8,128)(2,1)} %param.6) | data formatting | bytes 8388608 | tf_op args[1]
  13.0 0.0 copy-start.2
  13.0 6.8 %all-to-all-start = ((bf16[256,8,1024]{0,2,1:T(8,128)(2,1)}), bf16[256,8,1024]{0,2,1:T(8,128)(2,1)}, u32[]{:S(2)}, u32[]{:S(2)}) async-start(bf16[256,8,1024]{0,2,1:T(8,128)(2,1)} %bitcast.38), calls=%async_computation | async-start | bytes 8388608 | tf_op jit(solution)/shard_map/all_to_all | solution.py:21
  19.8 0.0 reduce-scatter.4.cloned.1.call-start
  19.8 0.0 copy-done.2
  19.9 3.4 %fusion.11 = f32[2048,16]{0,1:T(8,128)S(1)} fusion(bf16[2048,1024]{1,0:T(8,128)(2,1)} %param.5, bf16[1024,16]{0,1:T(8,128)(2,1)S(1)} %copy-done.2), kind=kOutput, calls=%fused_computation.20 | convolution fusion | flops 67108864 | bytes 4358144 | tf_op jit(solution)/shard_map/dot_general | solution.py:18
  23.2 70.1 %all-reduce.2 = bf16[2048,16]{0,1:T(8,128)(2,1)S(1)} all-reduce(f32[2048,16]{0,1:T(8,128)S(1)} %fusion.11), channel_id=1, replica_groups=mesh['dp'=32,'tensor'=8] {'tensor'}, use_global_device_ids=true, to_apply=%region_0.0 | all-reduce | flops 32768 | bytes 196608 | tf_op jit(solution)/shard_map/psum | solution.py:19
  93.3 0.0 all-to-all-done
  93.3 6.5 %copy.13 = bf16[8,256,1024]{2,1,0:T(8,128)(2,1)} copy(bf16[8,256,1024]{1,2,0:T(8,128)(2,1)} %bitcast.1) | data formatting | bytes 8388608 | tf_op jit(solution)/shard_map/all_to_all | solution.py:21
  99.8 0.0 copy-done
  99.8 3.0 %fusion = f32[2,16,512]{2,1,0:T(8,128)S(1)} fusion(bf16[2,1024,1024]{2,1,0:T(8,128)(2,1)} %bitcast.40, bf16[1024,512]{1,0:T(8,128)(2,1)S(1)} %copy-done, bf16[2,2,8,1024]{3,2,1,0:T(8,128)(2,1)S(1)} %bitcast.42), kind=kOutput, calls=%fused_computation.1 | convolution fusion | flops 100696064 | bytes 5373952 | tf_op jit(solution)/shard_map/erd,dk->erk/dot_general | solution.py:25
  102.8 0.0 copy-start.1
  102.8 2.6 %copy.18 = f32[2,16,512]{0,2,1:T(8,128)} copy(f32[2,16,512]{2,1,0:T(8,128)S(1)} %fusion) | data formatting | bytes 131072
  105.4 0.0 reduce-scatter.4.cloned.1.call-update
  105.4 55.8 %reduce-scatter.4.cloned.1.call-done = f32[1024,2]{1,0:T(8,128)} async-done(((f32[8192,2]{1,0:T(8,128)}), f32[1024,2]{1,0:T(8,128)}) %reduce-scatter.4.cloned.1.call-update) | async-done | bytes 8208
  161.2 1.2 copy.17
  162.5 42.2 %all-gather = f32[32,2,1024]{2,1,0:T(2,128)S(1)} all-gather(f32[1,2,1024]{2,1,0:T(2,128)S(1)} %bitcast.43), channel_id=1, replica_groups=mesh['dp'=32,'tensor'=8] {'dp'}, dimensions={0}, use_global_device_ids=true | all-gather | bytes 270336 | tf_op jit(solution)/shard_map/all_gather | solution.py:28
  204.6 0.2 reshape.28
  204.8 0.4 fusion.12
  205.2 0.0 copy-done.1
  205.2 0.4 convolution_bitcast_fusion
  205.6 32.9 %all-reduce = (f32[128,64]{0,1:T(8,128)S(1)}, f32[64,64]{1,0:T(8,128)S(1)}) all-reduce(f32[128,64]{0,1:T(8,128)S(1)} %convolution_bitcast_fusion, f32[64,64]{1,0:T(8,128)S(1)} %fusion.12), channel_id=1, replica_groups=mesh['dp'=32,'tensor'=8] {'tensor'}, use_global_device_ids=true, to_apply=%region_6.7 | all-reduce | flops 12288 | bytes 98304 | tf_op jit(solution)/shard_map/psum | solution.py:31
  238.5 0.6 select_reduce_fusion.1
  239.8 0.1 copy.15
  239.9 5.8 %cholesky.17 = f32[64,64]{1,0:T(8,128)S(1)} custom-call(f32[64,64]{1,0:T(8,128)S(1)} %fusion.10), custom_call_target="Cholesky" | custom-call | tf_op jit(solution)/shard_map/jit(cholesky)/cholesky | solution.py:35
  245.7 0.6 compare_reduce_fusion
  246.4 0.7 fusion.6
  247.0 4.9 %custom-call.8 = f32[1,64,64]{1,2,0:T(8,128)S(1)} custom-call(f32[1,64,64]{2,1,0:T(8,128)S(1)} %fusion.6), custom_call_target="InvertDiagBlocksLowerTriangular" | custom-call | tf_op jit(solution)/shard_map/triangular_solve | solution.py:14
  251.9 0.3 fusion.8
  252.2 0.8 convolution_multiply_fusion
  (3 shorter events, 0.1 us)
Async XLA Ops:
  6.5 93.3 %copy-start = (bf16[1024,512]{1,0:T(8,128)(2,1)S(1)}, bf16[1024,512]{1,0:T(8,128)(2,1)}, u32[]{:S(2)}) copy-start(bf16[1024,512]{1,0:T(8,128)(2,1)} %param.8) | copy-start | bytes 3145732
  13.0 6.8 %copy-start.2 = (bf16[1024,16]{0,1:T(8,128)(2,1)S(1)}, bf16[1024,16]{0,1:T(8,128)(2,1)}, u32[]{:S(2)}) copy-start(bf16[1024,16]{0,1:T(8,128)(2,1)} %param.7) | copy-start | bytes 98308
  13.0 80.3 %all-to-all-start = ((bf16[256,8,1024]{0,2,1:T(8,128)(2,1)}), bf16[256,8,1024]{0,2,1:T(8,128)(2,1)}, u32[]{:S(2)}, u32[]{:S(2)}) async-start(bf16[256,8,1024]{0,2,1:T(8,128)(2,1)} %bitcast.38), calls=%async_computation | async-start | bytes 8388608 | tf_op jit(solution)/shard_map/all_to_all | solution.py:21
  19.8 141.4 %reduce-scatter.4.cloned.1.call-start = ((), (), s32[]{:S(2)}) async-start(), calls=%async_computation.2 | async-start | bytes 4718592
  102.8 102.4 %copy-start.1 = (bf16[128,1024]{1,0:T(8,128)(2,1)S(1)}, bf16[128,1024]{1,0:T(8,128)(2,1)}, u32[]{:S(2)}) copy-start(bf16[128,1024]{1,0:T(8,128)(2,1)} %param.9) | copy-start | bytes 786436
Sparse Core Ops, SparseCore 0:
  105.5 55.6 reduce-scatter.3
where the time goes:
time: 260 us
  blocking collectives  145 us (56%)
  waiting for transfers between devices  55.8 us (21%)
  local copies, waits for them, and re-layouts  17 us (7%)
  between operations  14.1 us (5%)
  other arithmetic  12.7 us (5%)
  matrix products  8.16 us (3%)
  starting transfers between devices  6.84 us (3%)
    psum x1, blocking collectives, shards(): summed = lax.psum(partial_input_rows, 'tensor')  70.1 us
    unnamed x2, waiting for transfers between devices  55.8 us
    all_gather x1, blocking collectives, shards(): table = lax.all_gather(reduced, 'dp', axis=0, tiled=True)  42.2 us
    psum x1, blocking collectives, shards(): kernel, cross = lax.psum((kernel_part, cross_part), 'tensor')  32.9 us
    unnamed x10, local copies, waits for them, and re-layouts  10.5 us
    all_to_all x1, starting transfers between devices, shards(): lax.all_to_all(cotangent, 'tensor', split_axis=1, concat_axis=0, tiled=True)  6.84 us
    another operation x3, other arithmetic, shards(): factor = jnp.linalg.cholesky(damped_system)  6.52 us
    all_to_all x1, local copies, waits for them, and re-layouts, shards(): lax.all_to_all(cotangent, 'tensor', split_axis=1, concat_axis=0, tiled=True)  6.46 us
  transfers between devices with their start and end apart: 2, of which 1 were waited for; matrix products, arithmetic and copies ran while one was open for 1% of the time, Pallas kernels for 0%

commit v1 on v0

v1 whole, which is shorter than its diff:
```python
import functools

import jax
import jax.numpy as jnp
from jax import lax
from jax.experimental import pallas as pl
from jax.experimental.pallas import tpu as pltpu
from jax.sharding import PartitionSpec as P

RANK = 16
PK = 512
SEQS = 64
MESH = pl.DeviceIdType.MESH
HIGHEST = lax.Precision.HIGHEST
F32 = jnp.float32
BF16 = jnp.bfloat16

PARTNERS = ((1, 2), (1, 0), (1, 1), (1, 3), (0, 2), (0, 1), (0, 3))
DOUBLINGS = 7


def doubling_constants():
    t, c = 130.0 / 128.0, []
    for _ in range(DOUBLINGS):
        c.append(2 * t * t / (2 * t * t - 1))
        t = 2 * t * t - 1
    return c


def nt(a, b, precision=None):
    return lax.dot_general(
        a, b, (((1,), (1,)), ((), ())), precision=precision, preferred_element_type=F32
    )


def take(sem, like):
    pltpu.make_async_copy(like, like, sem).wait()


def kernel(
    acts, cot, down, proj, queries, out,
    acts_v, cot_v, down_v, proj_v, q_v,
    send1, recv1, send2, recv2, parts, send3, recv3, table,
    send_k, recv_k, send_c, recv_c, rows,
    load_sem, acts_sem, s_sem, r_sem,
):
    dp, me = lax.axis_index("dp"), lax.axis_index("tensor")
    x, y = me // 4, lax.rem(me, 4)
    core, spot = lax.rem(dp, 2), dp // 2
    sibling = dp + 1 - 2 * core

    def partner(dx, dy):
        return lax.rem(x + dx, 2) * 4 + lax.rem(y + dy, 4)

    def post(src, dst, stage, device):
        copy = pltpu.make_async_remote_copy(
            src_ref=src, dst_ref=dst, send_sem=s_sem.at[stage], recv_sem=r_sem.at[stage],
            device_id=device, device_id_type=MESH,
        )
        copy.start()

    loads = []

    def load(src, dst, sem):
        copy = pltpu.make_async_copy(src, dst, sem)
        copy.start()
        return copy

    order = [partner(dx, dy) for dx, dy in PARTNERS] + [me]
    down_copy = load(down, down_v, load_sem.at[0])
    acts_copies = []
    for i, p in enumerate(order):
        tokens = pl.ds(pl.multiple_of(p * 256, 256), 256)
        acts_copies.append(load(acts.at[tokens], acts_v.at[i], acts_sem.at[i]))
    for i in range(4):
        tokens = pl.ds(i * 64, 64)
        load(cot.at[tokens], cot_v.at[tokens], load_sem.at[1])
    proj_copy = load(proj, proj_v, load_sem.at[2])
    q_copy = load(queries, q_v, load_sem.at[3])

    barrier = pltpu.get_barrier_semaphore()
    for p in order[:-1]:
        pl.semaphore_signal(barrier, inc=1, device_id={"tensor": p}, device_id_type=MESH)
    pl.semaphore_signal(barrier, inc=1, device_id={"dp": sibling}, device_id_type=MESH)
    for k in range(1, 16):
        there = lax.rem(spot + k, 16) * 2 + core
        pl.semaphore_signal(barrier, inc=1, device_id={"dp": there}, device_id_type=MESH)

    down_copy.wait()
    down_t = down_v[...]
    for i, p in enumerate(order):
        acts_copies[i].wait()
        part = nt(down_t, acts_v[i])
        if i == 0:
            pl.semaphore_wait(barrier, 23)
        if i < 7:
            send1[i] = part
            post(send1.at[i], recv1.at[me], 0, {"tensor": p})
        else:
            recv1[me] = part
    take(r_sem.at[0], recv1.at[pl.ds(0, 7)])
    inputs = recv1[0]
    for t in range(1, 8):
        inputs = inputs + recv1[t]
    inputs = inputs.astype(BF16)

    take(load_sem.at[1], cot_v)
    own_rows = pl.ds(pl.multiple_of(me * 16, 16), 16)
    for i, p in enumerate(order):
        features = pl.ds(pl.multiple_of(p * 1024, 1024), 1024)
        grad = jnp.dot(inputs, cot_v[:, features], preferred_element_type=F32).astype(BF16)
        if i < 7:
            send2[i] = grad
            post(send2.at[i], recv2.at[own_rows], 1, {"tensor": p})
        else:
            recv2[own_rows, :] = grad
    proj_copy.wait()
    take(r_sem.at[1], recv2.at[pl.ds(0, 112)])

    projected = jnp.dot(recv2[...], proj_v[...], preferred_element_type=F32)
    for s in range(2):
        total = projected[64 * s:64 * s + 16]
        for t in range(1, 4):
            total = total + projected[64 * s + 16 * t:64 * s + 16 * t + 16]
        for q in range(4):
            parts[32 * q + 16 * s:32 * q + 16 * s + 16, :] = total[:, 128 * q:128 * q + 128]
    for s in range(2):
        for i in range(2):
            for q in range(4):
                send3[pl.ds(s * 8 + i * 4 + q, 8, stride=16), :] = parts[
                    pl.ds(32 * q + 16 * s + i, 8, stride=2), :
                ]
    for i, p in enumerate(order[:-1]):
        block = pl.ds(pl.multiple_of(p * 16, 16), 16)
        post(send3.at[block], recv3.at[me], 2, {"tensor": p})
    recv3[me] = send3[pl.ds(pl.multiple_of(me * 16, 16), 16), :]
    take(r_sem.at[2], recv3.at[pl.ds(0, 7)])
    mine = recv3[0]
    for t in range(1, 8):
        mine = mine + recv3[t]

    slot = pl.ds(pl.multiple_of(core * 256 + spot * 16, 16), 16)
    table[slot, :] = mine
    for k in range(1, 16):
        there = lax.rem(spot + k, 16) * 2 + core
        post(table.at[slot], table.at[slot], 3, {"dp": there})
    take(r_sem.at[3], table.at[pl.ds(0, 240)])
    half = pl.ds(pl.multiple_of(core * 256, 256), 256)
    post(table.at[half], table.at[half], 4, {"dp": sibling})
    q_copy.wait()
    take(r_sem.at[4], table.at[pl.ds(0, 256)])

    acc = None
    for i in range(4):
        pieces = [table[pl.ds(2 * i + j, 64, stride=8), :] for j in range(2)]
        rows_f = jnp.concatenate(pieces, axis=1)
        hi = rows_f.astype(BF16)
        lo = (rows_f - hi.astype(F32)).astype(BF16)
        both = jnp.concatenate([hi, lo], axis=0)
        right = jnp.concatenate([both, q_v[:, pl.ds(i * 256, 256)]], axis=0)
        term = nt(both, right)
        acc = term if acc is None else acc + term
    acc = acc[:64] + acc[64:]
    gram = acc[:, :128]
    gram = gram + pltpu.roll(gram, 64, 1)
    lane = lax.broadcasted_iota(jnp.int32, (32, 128), 1)
    gram = jnp.where(lane < 64, gram[:32], gram[32:])
    send_k[...] = gram
    for p in order[:-1]:
        post(send_k, recv_k.at[me], 5, {"tensor": p})
    send_c[...] = acc[:, 128:]
    for p in order[:-1]:
        post(send_c, recv_c.at[me], 6, {"tensor": p})
    recv_k[me] = gram
    recv_c[me] = acc[:, 128:]

    take(r_sem.at[5], recv_k.at[pl.ds(0, 7)])
    gram = recv_k[0]
    for t in range(1, 8):
        gram = gram + recv_k[t]
    gram = jnp.concatenate([gram, pltpu.roll(gram, 64, 1)], axis=0)[:, :64]
    eye = (
        lax.broadcasted_iota(jnp.int32, (64, 64), 0)
        == lax.broadcasted_iota(jnp.int32, (64, 64), 1)
    ).astype(F32)
    trace = jnp.sum(gram * eye, keepdims=True)
    unit = 128.0 / (65.0 * trace)
    w = (1.0 - 1.0 / 65.0) * eye - gram * unit
    inverse = eye + w
    scale = 64.0
    constants = doubling_constants()
    for j in range(DOUBLINGS):
        scale = scale * constants[j]
        if j:
            inverse = inverse + jnp.dot(inverse, w, precision=HIGHEST, preferred_element_type=F32)
        if j < DOUBLINGS - 1:
            square = jnp.dot(w, w, precision=HIGHEST, preferred_element_type=F32)
            w = constants[j] * square - (constants[j] - 1.0) * eye

    take(r_sem.at[6], recv_c.at[pl.ds(0, 7)])
    cross = recv_c[0]
    for t in range(1, 8):
        cross = cross + recv_c[t]
    cross = cross * (unit * scale)
    rows[...] = jnp.dot(inverse, cross, precision=HIGHEST, preferred_element_type=F32)
    pieces = []
    for c in range(2):
        for s in range(2):
            pieces.append(rows[pl.ds(c * 32 + s, 16, stride=2), :])
    for c in range(2):
        for s in range(2):
            out[pl.ds(c * 2 + s, 16, stride=4), :] = pieces[c * 2 + s]

    take(s_sem.at[0], send1.at[pl.ds(0, 7)])
    take(s_sem.at[1], send2.at[pl.ds(0, 7)])
    take(s_sem.at[2], send3.at[pl.ds(0, 112)])
    take(s_sem.at[3], table.at[pl.ds(0, 240)])
    take(s_sem.at[4], table.at[pl.ds(0, 256)])
    take(s_sem.at[5], recv_k.at[pl.ds(0, 7)])
    take(s_sem.at[6], recv_c.at[pl.ds(0, 7)])


def shards(acts, cotangent, down_weight, project, queries):
    v = pltpu.VMEM
    scores = pl.pallas_call(
        kernel,
        out_shape=jax.ShapeDtypeStruct((64, 128), F32),
        in_specs=[pl.BlockSpec(memory_space=pl.ANY)] * 5,
        out_specs=pl.BlockSpec(memory_space=pltpu.VMEM),
        scratch_shapes=[
            v((8, 256, 1024), BF16), v((256, 8192), BF16), v((16, 1024), BF16),
            v((1024, 512), BF16), v((128, 1024), BF16),
            v((8, 16, 256), F32), v((8, 16, 256), F32),
            v((8, 16, 1024), BF16), v((128, 1024), BF16),
            v((128, 128), F32), v((128, 128), F32), v((8, 16, 128), F32), v((512, 128), F32),
            v((32, 128), F32), v((8, 32, 128), F32), v((64, 128), F32), v((8, 64, 128), F32),
            v((64, 128), F32),
            pltpu.SemaphoreType.DMA((4,)), pltpu.SemaphoreType.DMA((8,)),
            pltpu.SemaphoreType.DMA((7,)), pltpu.SemaphoreType.DMA((7,)),
        ],
        compiler_params=pltpu.CompilerParams(
            collective_id=0, has_side_effects=True, vmem_limit_bytes=56 * 1024 * 1024
        ),
    )(acts, cotangent, down_weight.T, project, queries)
    return scores.T


def solution(mesh):
    placed = (
        P("dp", "tensor"),
        P(("dp", "tensor"), None),
        P("tensor", None),
        P("tensor", None),
        P("dp", "tensor"),
    )
    return jax.shard_map(
        shards, mesh=mesh, in_specs=placed, out_specs=P("dp", None), check_vma=False
    )
```

time: 260 us -> 41.9 us (0.16)
  the two profiles are of different devices: /device:TPU:2 before, /device:TPU:1 now
where the time goes in v1:
time: 41.9 us; the launch traced here: 41.8 us
  Pallas kernels  40.4 us (96%)
  local copies, waits for them, and re-layouts  1.38 us (3%)
    pallas_call x1, Pallas kernels, shards(): pl.pallas_call(kernel, out_shape=jax.ShapeDtypeStruct((64, 128), F32), in...  40.4 us
    unnamed x1, local copies, waits for them, and re-layouts  1.38 us

profile of v1, /device:TPU:1, one launch (start us, length us, event | category | flops | bytes accessed | tf_op | source)
XLA Modules:
  0.0 41.8 jit_solution(9419396184387608752)
XLA Ops:
  0.0 40.4 %shard_map.55 = f32[64,128]{1,0:T(8,128)} custom-call(bf16[2048,1024]{1,0:T(8,128)(2,1)} %acts.1, bf16[256,8192]{1,0:T(8,128)(2,1)} %cot.1, bf16[16,1024]{1,0:T(8,128)(2,1)} %bitcast.3, bf16[1024,512]{1,0:T(8,128)(2,1)} %proj.1, bf16[128,1024]{1,0:T(8,128)(2,1)} %queries.1), custom_call_target="tpu_custom_call" | custom-call | tf_op jit(solution)/shard_map/pallas_call | solution.py:225
  40.4 1.4 %copy.7 = f32[128,64]{0,1:T(8,128)} copy(f32[128,64]{0,1:T(8,128)} %bitcast.2) | data formatting | bytes 65536

commit v2 on v1

--- a/solution.py
+++ b/solution.py
@@ -15,7 +15,9 @@
 F32 = jnp.float32
 BF16 = jnp.bfloat16
 
-PARTNERS = ((1, 2), (1, 0), (1, 1), (1, 3), (0, 2), (0, 1), (0, 3))
+PARTNERS = ((1, 2), (1, 1), (1, 3), (0, 2), (1, 0), (0, 1), (0, 3))
+AWAY = (14, 13, 15, 12, 4, 11, 8, 3, 5, 10, 9, 2, 6, 1, 7)
+NEAR = 12
 DOUBLINGS = 7
 
 
@@ -33,6 +35,12 @@
     )
 
 
+def start(other, e):
+    if e < NEAR:
+        return 16 * (other * NEAR + e)
+    return 16 * (2 * NEAR + other * (16 - NEAR) + e - NEAR)
+
+
 def take(sem, like):
     pltpu.make_async_copy(like, like, sem).wait()
 
@@ -41,8 +49,8 @@
     acts, cot, down, proj, queries, out,
     acts_v, cot_v, down_v, proj_v, q_v,
     send1, recv1, send2, recv2, parts, send3, recv3, table,
-    send_k, recv_k, send_c, recv_c, rows,
-    load_sem, acts_sem, s_sem, r_sem,
+    send_k, recv_k, send_c, recv_c,
+    load_sem, acts_sem, s_sem, r_sem, relay,
 ):
     dp, me = lax.axis_index("dp"), lax.axis_index("tensor")
     x, y = me // 4, lax.rem(me, 4)
@@ -51,6 +59,9 @@
 
     def partner(dx, dy):
         return lax.rem(x + dx, 2) * 4 + lax.rem(y + dy, 4)
+
+    def along(dx, dz):
+        return lax.rem(spot // 8 + dx, 2) * 16 + lax.rem(spot + dz, 8) * 2 + core
 
     def post(src, dst, stage, device):
         copy = pltpu.make_async_remote_copy(
@@ -69,35 +80,50 @@
     order = [partner(dx, dy) for dx, dy in PARTNERS] + [me]
     down_copy = load(down, down_v, load_sem.at[0])
     acts_copies = []
-    for i, p in enumerate(order):
-        tokens = pl.ds(pl.multiple_of(p * 256, 256), 256)
-        acts_copies.append(load(acts.at[tokens], acts_v.at[i], acts_sem.at[i]))
+
+    def load_acts(i):
+        tokens = pl.ds(pl.multiple_of(order[i] * 256, 256), 256)
+        acts_copies.append(load(acts.at[tokens], acts_v.at[pl.ds(i * 256, 256)], acts_sem.at[i]))
+
     for i in range(4):
-        tokens = pl.ds(i * 64, 64)
-        load(cot.at[tokens], cot_v.at[tokens], load_sem.at[1])
-    proj_copy = load(proj, proj_v, load_sem.at[2])
-    q_copy = load(queries, q_v, load_sem.at[3])
+        load_acts(i)
 
     barrier = pltpu.get_barrier_semaphore()
     for p in order[:-1]:
         pl.semaphore_signal(barrier, inc=1, device_id={"tensor": p}, device_id_type=MESH)
     pl.semaphore_signal(barrier, inc=1, device_id={"dp": sibling}, device_id_type=MESH)
-    for k in range(1, 16):
-        there = lax.rem(spot + k, 16) * 2 + core
+    close = [along(1, 0)] + [along(0, dz) for dz in (2, 6, 1, 7)]
+    for there in close:
         pl.semaphore_signal(barrier, inc=1, device_id={"dp": there}, device_id_type=MESH)
+
+    for i in range(4, 8):
+        load_acts(i)
 
     down_copy.wait()
     down_t = down_v[...]
-    for i, p in enumerate(order):
-        acts_copies[i].wait()
-        part = nt(down_t, acts_v[i])
-        if i == 0:
-            pl.semaphore_wait(barrier, 23)
-        if i < 7:
-            send1[i] = part
-            post(send1.at[i], recv1.at[me], 0, {"tensor": p})
+    for pair in range(4):
+        acts_copies[2 * pair].wait()
+        acts_copies[2 * pair + 1].wait()
+        part = nt(down_t, acts_v[pl.ds(pair * 512, 512), :])
+        send1[2 * pair] = part[:, :256]
+        if pair < 3:
+            send1[2 * pair + 1] = part[:, 256:]
         else:
-            recv1[me] = part
+            recv1[me] = part[:, 256:]
+        if pair == 1:
+            for i in range(4):
+                tokens = pl.ds(i * 64, 64)
+                load(cot.at[tokens], cot_v.at[tokens], load_sem.at[1])
+            proj_copy = load(proj, proj_v, load_sem.at[2])
+            q_copy = load(queries, q_v, load_sem.at[3])
+            pl.semaphore_wait(barrier, 13)
+            for i in range(2):
+                post(send1.at[i], recv1.at[me], 0, {"tensor": order[i]})
+        if pair > 0:
+            for i in range(2 * pair, min(2 * pair + 2, 7)):
+                post(send1.at[i], recv1.at[me], 0, {"tensor": order[i]})
+    for dz in (2, 6):
+        pl.semaphore_signal(relay.at[0], inc=1, device_id={"dp": along(0, dz)}, device_id_type=MESH)
     take(r_sem.at[0], recv1.at[pl.ds(0, 7)])
     inputs = recv1[0]
     for t in range(1, 8):
@@ -114,6 +140,8 @@
             post(send2.at[i], recv2.at[own_rows], 1, {"tensor": p})
         else:
             recv2[own_rows, :] = grad
+    pl.semaphore_wait(relay.at[0], 2)
+    pl.semaphore_signal(relay.at[1], inc=1, device_id={"dp": along(1, 0)}, device_id_type=MESH)
     proj_copy.wait()
     take(r_sem.at[1], recv2.at[pl.ds(0, 112)])
 
@@ -139,16 +167,22 @@
     for t in range(1, 8):
         mine = mine + recv3[t]
 
-    slot = pl.ds(pl.multiple_of(core * 256 + spot * 16, 16), 16)
-    table[slot, :] = mine
-    for k in range(1, 16):
-        there = lax.rem(spot + k, 16) * 2 + core
-        post(table.at[slot], table.at[slot], 3, {"dp": there})
-    take(r_sem.at[3], table.at[pl.ds(0, 240)])
-    half = pl.ds(pl.multiple_of(core * 256, 256), 256)
-    post(table.at[half], table.at[half], 4, {"dp": sibling})
+    table[0:16, :] = mine
+    pl.semaphore_wait(relay.at[1], 1)
+    for e in AWAY:
+        back = 8 - e if e < 8 else 8 + (20 - e) % 8
+        there = along(e // 8, (e - 2 * (e // 8)) % 8)
+        block = table.at[pl.ds(start(0, back), 16)]
+        post(table.at[pl.ds(0, 16)], block, 3 if back >= NEAR else 4, {"dp": there})
+    take(r_sem.at[4], table.at[pl.ds(0, 16 * (NEAR - 1))])
+    near = pl.ds(0, 16 * NEAR)
+    post(table.at[near], table.at[pl.ds(start(1, 0), 16 * NEAR)], 7, {"dp": sibling})
     q_copy.wait()
-    take(r_sem.at[4], table.at[pl.ds(0, 256)])
+    take(r_sem.at[3], table.at[pl.ds(0, 16 * (16 - NEAR))])
+    far = pl.ds(start(0, NEAR), 16 * (16 - NEAR))
+    post(table.at[far], table.at[pl.ds(start(1, NEAR), 16 * (16 - NEAR))], 8, {"dp": sibling})
+    take(r_sem.at[7], table.at[near])
+    take(r_sem.at[8], table.at[far])
 
     acc = None
     for i in range(4):
@@ -168,11 +202,11 @@
     send_k[...] = gram
     for p in order[:-1]:
         post(send_k, recv_k.at[me], 5, {"tensor": p})
-    send_c[...] = acc[:, 128:]
+    send_c[...] = acc[:, 128:].astype(BF16)
     for p in order[:-1]:
         post(send_c, recv_c.at[me], 6, {"tensor": p})
     recv_k[me] = gram
-    recv_c[me] = acc[:, 128:]
+    recv_c[me] = acc[:, 128:].astype(BF16)
 
     take(r_sem.at[5], recv_k.at[pl.ds(0, 7)])
     gram = recv_k[0]
@@ -187,56 +221,62 @@
     unit = 128.0 / (65.0 * trace)
     w = (1.0 - 1.0 / 65.0) * eye - gram * unit
     inverse = eye + w
+    row = lax.broadcasted_iota(jnp.int32, (64, 64), 0)
+    column = lax.broadcasted_iota(jnp.int32, (64, 64), 1)
+    block = column // 2
+    near_block = block < 2 * NEAR
+    other = jnp.where(near_block, block // NEAR, (block - 2 * NEAR) // (16 - NEAR))
+    e = jnp.where(near_block, lax.rem(block, NEAR), NEAR + lax.rem(block, 16 - NEAR))
+    dx = e // 8
+    place = lax.rem(spot // 8 + dx, 2) * 32 + lax.rem(lax.rem(spot, 8) + e - 2 * dx + 8, 8) * 4
+    place = place + lax.rem(core + other, 2) * 2 + lax.rem(column, 2)
+    place = (place == row).astype(F32)
     scale = 64.0
     constants = doubling_constants()
     for j in range(DOUBLINGS):
         scale = scale * constants[j]
         if j:
-            inverse = inverse + jnp.dot(inverse, w, precision=HIGHEST, preferred_element_type=F32)
+            inverse = inverse + jnp.dot(inverse, w, precision=lax.Precision.HIGH, preferred_element_type=F32)
         if j < DOUBLINGS - 1:
-            square = jnp.dot(w, w, precision=HIGHEST, preferred_element_type=F32)
+            square = jnp.dot(w, w, precision=lax.Precision.HIGH, preferred_element_type=F32)
             w = constants[j] * square - (constants[j] - 1.0) * eye
 
+    inverse = jnp.dot(place, inverse * (unit * scale), precision=lax.Precision.HIGH, preferred_element_type=F32)
+
     take(r_sem.at[6], recv_c.at[pl.ds(0, 7)])
-    cross = recv_c[0]
-    for t in range(1, 8):
-        cross = cross + recv_c[t]
-    cross = cross * (unit * scale)
-    rows[...] = jnp.dot(inverse, cross, precision=HIGHEST, preferred_element_type=F32)
-    pieces = []
-    for c in range(2):
-        for s in range(2):
-            pieces.append(rows[pl.ds(c * 32 + s, 16, stride=2), :])
-    for c in range(2):
-        for s in range(2):
-            out[pl.ds(c * 2 + s, 16, stride=4), :] = pieces[c * 2 + s]
+    cross = recv_c[0].astype(F32)
+    for t in range(1, 8):
+        cross = cross + recv_c[t].astype(F32)
+    out[...] = jnp.dot(inverse, cross, precision=lax.Precision.HIGH, preferred_element_type=F32)
 
     take(s_sem.at[0], send1.at[pl.ds(0, 7)])
     take(s_sem.at[1], send2.at[pl.ds(0, 7)])
     take(s_sem.at[2], send3.at[pl.ds(0, 112)])
-    take(s_sem.at[3], table.at[pl.ds(0, 240)])
-    take(s_sem.at[4], table.at[pl.ds(0, 256)])
+    take(s_sem.at[3], table.at[pl.ds(0, 16 * (16 - NEAR))])
+    take(s_sem.at[4], table.at[pl.ds(0, 16 * (NEAR - 1))])
     take(s_sem.at[5], recv_k.at[pl.ds(0, 7)])
     take(s_sem.at[6], recv_c.at[pl.ds(0, 7)])
+    take(s_sem.at[7], table.at[near])
+    take(s_sem.at[8], table.at[far])
 
 
 def shards(acts, cotangent, down_weight, project, queries):
     v = pltpu.VMEM
     scores = pl.pallas_call(
         kernel,
-        out_shape=jax.ShapeDtypeStruct((64, 128), F32),
+        out_shape=pltpu.VMEM((64, 128), F32),
         in_specs=[pl.BlockSpec(memory_space=pl.ANY)] * 5,
         out_specs=pl.BlockSpec(memory_space=pltpu.VMEM),
         scratch_shapes=[
-            v((8, 256, 1024), BF16), v((256, 8192), BF16), v((16, 1024), BF16),
+            v((2048, 1024), BF16), v((256, 8192), BF16), v((16, 1024), BF16),
             v((1024, 512), BF16), v((128, 1024), BF16),
             v((8, 16, 256), F32), v((8, 16, 256), F32),
             v((8, 16, 1024), BF16), v((128, 1024), BF16),
             v((128, 128), F32), v((128, 128), F32), v((8, 16, 128), F32), v((512, 128), F32),
-            v((32, 128), F32), v((8, 32, 128), F32), v((64, 128), F32), v((8, 64, 128), F32),
-            v((64, 128), F32),
+            v((32, 128), F32), v((8, 32, 128), F32), v((64, 128), BF16), v((8, 64, 128), BF16),
             pltpu.SemaphoreType.DMA((4,)), pltpu.SemaphoreType.DMA((8,)),
-            pltpu.SemaphoreType.DMA((7,)), pltpu.SemaphoreType.DMA((7,)),
+            pltpu.SemaphoreType.DMA((9,)), pltpu.SemaphoreType.DMA((9,)),
+            pltpu.SemaphoreType.REGULAR((2,)),
         ],
         compiler_params=pltpu.CompilerParams(
             collective_id=0, has_side_effects=True, vmem_limit_bytes=56 * 1024 * 1024

time: 41.9 us -> 38.3 us (0.914)
  Pallas kernels: 40.4 us -> 37.6 us
  local copies, waits for them, and re-layouts: 1.38 us -> 0.62 us
    pallas_call x1, Pallas kernels: 40.4 us -> 37.6 us  [shards(): pl.pallas_call(kernel, out_shape=pltpu.VMEM((64, 128), F32), in_specs=[pl...]
    unnamed x1, local copies, waits for them, and re-layouts: 1.38 us -> 0.62 us
where the time goes in v2:
time: 38.3 us; the launch traced here: 38.2 us
  Pallas kernels  37.6 us (98%)
  local copies, waits for them, and re-layouts  0.62 us (2%)
    pallas_call x1, Pallas kernels, shards(): pl.pallas_call(kernel, out_shape=pltpu.VMEM((64, 128), F32), in_specs=[pl...  37.6 us

profile of v2, /device:TPU:1, one launch (start us, length us, event | category | flops | bytes accessed | tf_op | source)
XLA Modules:
  0.0 38.2 jit_solution(17693063824173924799)
XLA Ops:
  0.0 37.6 %shard_map.55 = f32[64,128]{1,0:T(8,128)S(1)} custom-call(bf16[2048,1024]{1,0:T(8,128)(2,1)} %acts.1, bf16[256,8192]{1,0:T(8,128)(2,1)} %cot.1, bf16[16,1024]{1,0:T(8,128)(2,1)} %bitcast.3, bf16[1024,512]{1,0:T(8,128)(2,1)} %proj.1, bf16[128,1024]{1,0:T(8,128)(2,1)} %queries.1), custom_call_target="tpu_custom_call" | custom-call | tf_op jit(solution)/shard_map/pallas_call | solution.py:265
  37.6 0.6 %copy.7 = f32[128,64]{0,1:T(8,128)} copy(f32[128,64]{0,1:T(8,128)S(1)} %bitcast.2) | data formatting | bytes 65536

commit v3 on v2

--- a/solution.py
+++ b/solution.py
@@ -11,13 +11,12 @@
 PK = 512
 SEQS = 64
 MESH = pl.DeviceIdType.MESH
-HIGHEST = lax.Precision.HIGHEST
 F32 = jnp.float32
 BF16 = jnp.bfloat16
 
 PARTNERS = ((1, 2), (1, 1), (1, 3), (0, 2), (1, 0), (0, 1), (0, 3))
 AWAY = (14, 13, 15, 12, 4, 11, 8, 3, 5, 10, 9, 2, 6, 1, 7)
-NEAR = 12
+NEAR = 13
 DOUBLINGS = 7
 
 
@@ -29,9 +28,9 @@
     return c
 
 
-def nt(a, b, precision=None):
+def nt(a, b):
     return lax.dot_general(
-        a, b, (((1,), (1,)), ((), ())), precision=precision, preferred_element_type=F32
+        a, b, (((1,), (1,)), ((), ())), preferred_element_type=F32
     )
 
 
@@ -41,6 +40,26 @@
     return 16 * (2 * NEAR + other * (16 - NEAR) + e - NEAR)
 
 
+def split(a):
+    high = a.astype(BF16)
+    return high, (a - high.astype(F32)).astype(BF16)
+
+
+def product(lefts, right):
+    rows = []
+    for left in lefts:
+        high, low = split(left)
+        lane = lax.broadcasted_iota(jnp.int32, left.shape, 1)
+        rows.append(jnp.where(lane < 64, high, low))
+    left = jnp.concatenate(rows, axis=0)
+    high, low = split(right)
+    return jnp.dot(
+        jnp.concatenate([left, left], axis=1),
+        jnp.concatenate([high, high, low, low], axis=0),
+        preferred_element_type=F32,
+    )
+
+
 def take(sem, like):
     pltpu.make_async_copy(like, like, sem).wait()
 
@@ -48,7 +67,7 @@
 def kernel(
     acts, cot, down, proj, queries, out,
     acts_v, cot_v, down_v, proj_v, q_v,
-    send1, recv1, send2, recv2, parts, send3, recv3, table,
+    send1, recv1, send2, recv2, parts, send3, recv3, table, wide,
     send_k, recv_k, send_c, recv_c,
     load_sem, acts_sem, s_sem, r_sem, relay,
 ):
@@ -142,6 +161,8 @@
             recv2[own_rows, :] = grad
     pl.semaphore_wait(relay.at[0], 2)
     pl.semaphore_signal(relay.at[1], inc=1, device_id={"dp": along(1, 0)}, device_id_type=MESH)
+    pl.semaphore_wait(relay.at[1], 1)
+    pl.semaphore_signal(relay.at[2], inc=1, device_id={"dp": sibling}, device_id_type=MESH)
     proj_copy.wait()
     take(r_sem.at[1], recv2.at[pl.ds(0, 112)])
 
@@ -167,36 +188,29 @@
     for t in range(1, 8):
         mine = mine + recv3[t]
 
-    table[0:16, :] = mine
-    pl.semaphore_wait(relay.at[1], 1)
+    table[0:16, :] = mine.astype(BF16)
+    pl.semaphore_wait(relay.at[2], 1)
     for e in AWAY:
         back = 8 - e if e < 8 else 8 + (20 - e) % 8
         there = along(e // 8, (e - 2 * (e // 8)) % 8)
-        block = table.at[pl.ds(start(0, back), 16)]
-        post(table.at[pl.ds(0, 16)], block, 3 if back >= NEAR else 4, {"dp": there})
+        own = table.at[pl.ds(0, 16)]
+        post(own, table.at[pl.ds(start(0, back), 16)], 3 if e >= NEAR else 4, {"dp": there})
+        if e >= NEAR:
+            post(own, table.at[pl.ds(start(1, back), 16)], 3, {"dp": there + 1 - 2 * core})
     take(r_sem.at[4], table.at[pl.ds(0, 16 * (NEAR - 1))])
     near = pl.ds(0, 16 * NEAR)
     post(table.at[near], table.at[pl.ds(start(1, 0), 16 * NEAR)], 7, {"dp": sibling})
     q_copy.wait()
-    take(r_sem.at[3], table.at[pl.ds(0, 16 * (16 - NEAR))])
-    far = pl.ds(start(0, NEAR), 16 * (16 - NEAR))
-    post(table.at[far], table.at[pl.ds(start(1, NEAR), 16 * (16 - NEAR))], 8, {"dp": sibling})
     take(r_sem.at[7], table.at[near])
-    take(r_sem.at[8], table.at[far])
-
-    acc = None
-    for i in range(4):
-        pieces = [table[pl.ds(2 * i + j, 64, stride=8), :] for j in range(2)]
-        rows_f = jnp.concatenate(pieces, axis=1)
-        hi = rows_f.astype(BF16)
-        lo = (rows_f - hi.astype(F32)).astype(BF16)
-        both = jnp.concatenate([hi, lo], axis=0)
-        right = jnp.concatenate([both, q_v[:, pl.ds(i * 256, 256)]], axis=0)
-        term = nt(both, right)
-        acc = term if acc is None else acc + term
-    acc = acc[:64] + acc[64:]
+    both_near, far = pl.ds(0, 32 * NEAR), pl.ds(32 * NEAR, 32 * (16 - NEAR))
+    wide[both_near, :] = table[both_near, :].astype(F32)
+    take(r_sem.at[3], table.at[far])
+    wide[far, :] = table[far, :].astype(F32)
+
+    pieces = [wide[pl.ds(j, 64, stride=8), :].astype(BF16) for j in range(8)]
+    whole = jnp.concatenate(pieces, axis=1)
+    acc = nt(whole, jnp.concatenate([whole, whole, q_v[...]], axis=0))
     gram = acc[:, :128]
-    gram = gram + pltpu.roll(gram, 64, 1)
     lane = lax.broadcasted_iota(jnp.int32, (32, 128), 1)
     gram = jnp.where(lane < 64, gram[:32], gram[32:])
     send_k[...] = gram
@@ -212,52 +226,52 @@
     gram = recv_k[0]
     for t in range(1, 8):
         gram = gram + recv_k[t]
-    gram = jnp.concatenate([gram, pltpu.roll(gram, 64, 1)], axis=0)[:, :64]
-    eye = (
-        lax.broadcasted_iota(jnp.int32, (64, 64), 0)
-        == lax.broadcasted_iota(jnp.int32, (64, 64), 1)
-    ).astype(F32)
-    trace = jnp.sum(gram * eye, keepdims=True)
-    unit = 128.0 / (65.0 * trace)
+    turned = pltpu.roll(gram, 64, 1)
+    gram = jnp.concatenate(
+        [jnp.where(lane < 64, gram, turned), jnp.where(lane < 64, turned, gram)], axis=0
+    )
+    row = lax.broadcasted_iota(jnp.int32, (64, 128), 0)
+    column = lax.rem(lax.broadcasted_iota(jnp.int32, (64, 128), 1), 64)
+    eye = (row == column).astype(F32)
+    unit = 256.0 / (65.0 * jnp.sum(gram * eye, keepdims=True))
     w = (1.0 - 1.0 / 65.0) * eye - gram * unit
-    inverse = eye + w
-    row = lax.broadcasted_iota(jnp.int32, (64, 64), 0)
-    column = lax.broadcasted_iota(jnp.int32, (64, 64), 1)
     block = column // 2
     near_block = block < 2 * NEAR
     other = jnp.where(near_block, block // NEAR, (block - 2 * NEAR) // (16 - NEAR))
-    e = jnp.where(near_block, lax.rem(block, NEAR), NEAR + lax.rem(block, 16 - NEAR))
+    e = jnp.where(
+        near_block, lax.rem(block, NEAR), NEAR + lax.rem(block - 2 * NEAR + 16 - NEAR, 16 - NEAR)
+    )
     dx = e // 8
     place = lax.rem(spot // 8 + dx, 2) * 32 + lax.rem(lax.rem(spot, 8) + e - 2 * dx + 8, 8) * 4
     place = place + lax.rem(core + other, 2) * 2 + lax.rem(column, 2)
     place = (place == row).astype(F32)
+    inverse = place
     scale = 64.0
     constants = doubling_constants()
     for j in range(DOUBLINGS):
         scale = scale * constants[j]
-        if j:
-            inverse = inverse + jnp.dot(inverse, w, precision=lax.Precision.HIGH, preferred_element_type=F32)
         if j < DOUBLINGS - 1:
-            square = jnp.dot(w, w, precision=lax.Precision.HIGH, preferred_element_type=F32)
-            w = constants[j] * square - (constants[j] - 1.0) * eye
-
-    inverse = jnp.dot(place, inverse * (unit * scale), precision=lax.Precision.HIGH, preferred_element_type=F32)
+            products = product([w, inverse], w)
+            inverse = inverse + products[64:]
+            w = constants[j] * products[:64] - (constants[j] - 1.0) * eye
+        else:
+            inverse = inverse + product([inverse], w)
+    inverse = inverse * (unit * scale)
 
     take(r_sem.at[6], recv_c.at[pl.ds(0, 7)])
     cross = recv_c[0].astype(F32)
     for t in range(1, 8):
         cross = cross + recv_c[t].astype(F32)
-    out[...] = jnp.dot(inverse, cross, precision=lax.Precision.HIGH, preferred_element_type=F32)
+    out[...] = product([inverse], cross)
 
     take(s_sem.at[0], send1.at[pl.ds(0, 7)])
     take(s_sem.at[1], send2.at[pl.ds(0, 7)])
     take(s_sem.at[2], send3.at[pl.ds(0, 112)])
-    take(s_sem.at[3], table.at[pl.ds(0, 16 * (16 - NEAR))])
+    take(s_sem.at[3], table.at[far])
     take(s_sem.at[4], table.at[pl.ds(0, 16 * (NEAR - 1))])
     take(s_sem.at[5], recv_k.at[pl.ds(0, 7)])
     take(s_sem.at[6], recv_c.at[pl.ds(0, 7)])
     take(s_sem.at[7], table.at[near])
-    take(s_sem.at[8], table.at[far])
 
 
 def shards(acts, cotangent, down_weight, project, queries):
@@ -272,11 +286,11 @@
             v((1024, 512), BF16), v((128, 1024), BF16),
             v((8, 16, 256), F32), v((8, 16, 256), F32),
             v((8, 16, 1024), BF16), v((128, 1024), BF16),
-            v((128, 128), F32), v((128, 128), F32), v((8, 16, 128), F32), v((512, 128), F32),
+            v((128, 128), F32), v((128, 128), F32), v((8, 16, 128), F32), v((512, 128), BF16), v((512, 128), F32),
             v((32, 128), F32), v((8, 32, 128), F32), v((64, 128), BF16), v((8, 64, 128), BF16),
             pltpu.SemaphoreType.DMA((4,)), pltpu.SemaphoreType.DMA((8,)),
-            pltpu.SemaphoreType.DMA((9,)), pltpu.SemaphoreType.DMA((9,)),
-            pltpu.SemaphoreType.REGULAR((2,)),
+            pltpu.SemaphoreType.DMA((8,)), pltpu.SemaphoreType.DMA((8,)),
+            pltpu.SemaphoreType.REGULAR((3,)),
         ],
         compiler_params=pltpu.CompilerParams(
             collective_id=0, has_side_effects=True, vmem_limit_bytes=56 * 1024 * 1024

time: 38.3 us -> 37.2 us (0.971)
  Pallas kernels: 37.6 us -> 36.5 us
    pallas_call x1, Pallas kernels: 37.6 us -> 36.5 us  [shards(): pl.pallas_call(kernel, out_shape=pltpu.VMEM((64, 128), F32), in_specs=[pl...]
where the time goes in v3:
time: 37.2 us; the launch traced here: 37.1 us
  Pallas kernels  36.5 us (98%)
  local copies, waits for them, and re-layouts  0.62 us (2%)
    pallas_call x1, Pallas kernels, shards(): pl.pallas_call(kernel, out_shape=pltpu.VMEM((64, 128), F32), in_specs=[pl...  36.5 us

profile of v3, /device:TPU:1, one launch (start us, length us, event | category | flops | bytes accessed | tf_op | source)
XLA Modules:
  0.0 37.1 jit_solution(16089301568926315200)
XLA Ops:
  0.0 36.5 %shard_map.55 = f32[64,128]{1,0:T(8,128)S(1)} custom-call(bf16[2048,1024]{1,0:T(8,128)(2,1)} %acts.1, bf16[256,8192]{1,0:T(8,128)(2,1)} %cot.1, bf16[16,1024]{1,0:T(8,128)(2,1)} %bitcast.3, bf16[1024,512]{1,0:T(8,128)(2,1)} %proj.1, bf16[128,1024]{1,0:T(8,128)(2,1)} %queries.1), custom_call_target="tpu_custom_call" | custom-call | tf_op jit(solution)/shard_map/pallas_call | solution.py:279
  36.5 0.6 %copy.7 = f32[128,64]{0,1:T(8,128)} copy(f32[128,64]{0,1:T(8,128)S(1)} %bitcast.2) | data formatting | bytes 65536

commit v4 on v3

--- a/solution.py
+++ b/solution.py
@@ -14,7 +14,7 @@
 F32 = jnp.float32
 BF16 = jnp.bfloat16
 
-PARTNERS = ((1, 2), (1, 1), (1, 3), (0, 2), (1, 0), (0, 1), (0, 3))
+PARTNERS = ((1, 2), (0, 2), (1, 1), (1, 3), (0, 1), (1, 0), (0, 3))
 AWAY = (14, 13, 15, 12, 4, 11, 8, 3, 5, 10, 9, 2, 6, 1, 7)
 NEAR = 13
 DOUBLINGS = 7
@@ -209,18 +209,18 @@
 
     pieces = [wide[pl.ds(j, 64, stride=8), :].astype(BF16) for j in range(8)]
     whole = jnp.concatenate(pieces, axis=1)
-    acc = nt(whole, jnp.concatenate([whole, whole, q_v[...]], axis=0))
-    gram = acc[:, :128]
+    gram = nt(whole, jnp.concatenate([whole, whole], axis=0))
     lane = lax.broadcasted_iota(jnp.int32, (32, 128), 1)
     gram = jnp.where(lane < 64, gram[:32], gram[32:])
     send_k[...] = gram
     for p in order[:-1]:
         post(send_k, recv_k.at[me], 5, {"tensor": p})
-    send_c[...] = acc[:, 128:].astype(BF16)
+    recv_k[me] = gram
+    cross = nt(whole, q_v[...]).astype(BF16)
+    send_c[...] = cross
     for p in order[:-1]:
         post(send_c, recv_c.at[me], 6, {"tensor": p})
-    recv_k[me] = gram
-    recv_c[me] = acc[:, 128:].astype(BF16)
+    recv_c[me] = cross
 
     take(r_sem.at[5], recv_k.at[pl.ds(0, 7)])
     gram = recv_k[0]
@@ -258,20 +258,20 @@
             inverse = inverse + product([inverse], w)
     inverse = inverse * (unit * scale)
 
+    take(s_sem.at[0], send1.at[pl.ds(0, 7)])
+    take(s_sem.at[1], send2.at[pl.ds(0, 7)])
+    take(s_sem.at[2], send3.at[pl.ds(0, 112)])
+    take(s_sem.at[3], table.at[far])
+    take(s_sem.at[4], table.at[pl.ds(0, 16 * (NEAR - 1))])
+    take(s_sem.at[7], table.at[near])
+
     take(r_sem.at[6], recv_c.at[pl.ds(0, 7)])
     cross = recv_c[0].astype(F32)
     for t in range(1, 8):
         cross = cross + recv_c[t].astype(F32)
     out[...] = product([inverse], cross)
-
-    take(s_sem.at[0], send1.at[pl.ds(0, 7)])
-    take(s_sem.at[1], send2.at[pl.ds(0, 7)])
-    take(s_sem.at[2], send3.at[pl.ds(0, 112)])
-    take(s_sem.at[3], table.at[far])
-    take(s_sem.at[4], table.at[pl.ds(0, 16 * (NEAR - 1))])
     take(s_sem.at[5], recv_k.at[pl.ds(0, 7)])
     take(s_sem.at[6], recv_c.at[pl.ds(0, 7)])
-    take(s_sem.at[7], table.at[near])
 
 
 def shards(acts, cotangent, down_weight, project, queries):

time: 37.2 us -> 36.6 us (0.984)
  Pallas kernels: 36.5 us -> 35.9 us
    pallas_call x1, Pallas kernels: 36.5 us -> 35.9 us  [shards(): pl.pallas_call(kernel, out_shape=pltpu.VMEM((64, 128), F32), in_specs=[pl...]
where the time goes in v4:
time: 36.6 us; the launch traced here: 36.5 us
  Pallas kernels  35.9 us (98%)
  local copies, waits for them, and re-layouts  0.62 us (2%)
    pallas_call x1, Pallas kernels, shards(): pl.pallas_call(kernel, out_shape=pltpu.VMEM((64, 128), F32), in_specs=[pl...  35.9 us

profile of v4, /device:TPU:1, one launch (start us, length us, event | category | flops | bytes accessed | tf_op | source)
XLA Modules:
  0.0 36.5 jit_solution(2623815347138460518)
XLA Ops:
  0.0 35.9 %shard_map.55 = f32[64,128]{1,0:T(8,128)S(1)} custom-call(bf16[2048,1024]{1,0:T(8,128)(2,1)} %acts.1, bf16[256,8192]{1,0:T(8,128)(2,1)} %cot.1, bf16[16,1024]{1,0:T(8,128)(2,1)} %bitcast.3, bf16[1024,512]{1,0:T(8,128)(2,1)} %proj.1, bf16[128,1024]{1,0:T(8,128)(2,1)} %queries.1), custom_call_target="tpu_custom_call" | custom-call | tf_op jit(solution)/shard_map/pallas_call | solution.py:279
  35.9 0.6 %copy.7 = f32[128,64]{0,1:T(8,128)} copy(f32[128,64]{0,1:T(8,128)S(1)} %bitcast.2) | data formatting | bytes 65536

commit v5 on v4

--- a/solution.py
+++ b/solution.py
@@ -190,18 +190,17 @@
 
     table[0:16, :] = mine.astype(BF16)
     pl.semaphore_wait(relay.at[2], 1)
+    own = table.at[pl.ds(0, 16)]
+    near = pl.ds(0, 16 * NEAR)
     for e in AWAY:
         back = 8 - e if e < 8 else 8 + (20 - e) % 8
         there = along(e // 8, (e - 2 * (e // 8)) % 8)
-        own = table.at[pl.ds(0, 16)]
-        post(own, table.at[pl.ds(start(0, back), 16)], 3 if e >= NEAR else 4, {"dp": there})
-        if e >= NEAR:
-            post(own, table.at[pl.ds(start(1, back), 16)], 3, {"dp": there + 1 - 2 * core})
-    take(r_sem.at[4], table.at[pl.ds(0, 16 * (NEAR - 1))])
-    near = pl.ds(0, 16 * NEAR)
-    post(table.at[near], table.at[pl.ds(start(1, 0), 16 * NEAR)], 7, {"dp": sibling})
+        stage = 3 if e >= NEAR else 4
+        post(own, table.at[pl.ds(start(0, back), 16)], stage, {"dp": there})
+        post(own, table.at[pl.ds(start(1, back), 16)], stage, {"dp": there + 1 - 2 * core})
+    post(own, table.at[pl.ds(start(1, 0), 16)], 4, {"dp": sibling})
+    take(r_sem.at[4], table.at[pl.ds(0, 16 * (2 * NEAR - 1))])
     q_copy.wait()
-    take(r_sem.at[7], table.at[near])
     both_near, far = pl.ds(0, 32 * NEAR), pl.ds(32 * NEAR, 32 * (16 - NEAR))
     wide[both_near, :] = table[both_near, :].astype(F32)
     take(r_sem.at[3], table.at[far])
@@ -262,8 +261,7 @@
     take(s_sem.at[1], send2.at[pl.ds(0, 7)])
     take(s_sem.at[2], send3.at[pl.ds(0, 112)])
     take(s_sem.at[3], table.at[far])
-    take(s_sem.at[4], table.at[pl.ds(0, 16 * (NEAR - 1))])
-    take(s_sem.at[7], table.at[near])
+    take(s_sem.at[4], table.at[pl.ds(0, 16 * (2 * NEAR - 1))])
 
     take(r_sem.at[6], recv_c.at[pl.ds(0, 7)])
     cross = recv_c[0].astype(F32)

time: 36.6 us -> 35.5 us (0.970)
  Pallas kernels: 35.9 us -> 34.8 us
    pallas_call x1, Pallas kernels: 35.9 us -> 34.8 us  [shards(): pl.pallas_call(kernel, out_shape=pltpu.VMEM((64, 128), F32), in_specs=[pl...]
where the time goes in v5:
time: 35.5 us; the launch traced here: 35.4 us
  Pallas kernels  34.8 us (98%)
  local copies, waits for them, and re-layouts  0.62 us (2%)
    pallas_call x1, Pallas kernels, shards(): pl.pallas_call(kernel, out_shape=pltpu.VMEM((64, 128), F32), in_specs=[pl...  34.8 us

profile of v5, /device:TPU:1, one launch (start us, length us, event | category | flops | bytes accessed | tf_op | source)
XLA Modules:
  0.0 35.4 jit_solution(5506726908672631820)
XLA Ops:
  0.0 34.8 %shard_map.55 = f32[64,128]{1,0:T(8,128)S(1)} custom-call(bf16[2048,1024]{1,0:T(8,128)(2,1)} %acts.1, bf16[256,8192]{1,0:T(8,128)(2,1)} %cot.1, bf16[16,1024]{1,0:T(8,128)(2,1)} %bitcast.3, bf16[1024,512]{1,0:T(8,128)(2,1)} %proj.1, bf16[128,1024]{1,0:T(8,128)(2,1)} %queries.1), custom_call_target="tpu_custom_call" | custom-call | tf_op jit(solution)/shard_map/pallas_call | solution.py:277
  34.8 0.6 %copy.7 = f32[128,64]{0,1:T(8,128)} copy(f32[128,64]{0,1:T(8,128)S(1)} %bitcast.2) | data formatting | bytes 65536

commit v6 on v5

--- a/solution.py
+++ b/solution.py
@@ -14,7 +14,7 @@
 F32 = jnp.float32
 BF16 = jnp.bfloat16
 
-PARTNERS = ((1, 2), (0, 2), (1, 1), (1, 3), (0, 1), (1, 0), (0, 3))
+PARTNERS = ((0, 2), (1, 2), (0, 1), (1, 1), (1, 3), (0, 3), (1, 0))
 AWAY = (14, 13, 15, 12, 4, 11, 8, 3, 5, 10, 9, 2, 6, 1, 7)
 NEAR = 13
 DOUBLINGS = 7
@@ -196,8 +196,8 @@
         back = 8 - e if e < 8 else 8 + (20 - e) % 8
         there = along(e // 8, (e - 2 * (e // 8)) % 8)
         stage = 3 if e >= NEAR else 4
+        post(own, table.at[pl.ds(start(1, back), 16)], stage, {"dp": there + 1 - 2 * core})
         post(own, table.at[pl.ds(start(0, back), 16)], stage, {"dp": there})
-        post(own, table.at[pl.ds(start(1, back), 16)], stage, {"dp": there + 1 - 2 * core})
     post(own, table.at[pl.ds(start(1, 0), 16)], 4, {"dp": sibling})
     take(r_sem.at[4], table.at[pl.ds(0, 16 * (2 * NEAR - 1))])
     q_copy.wait()

time: 35.5 us -> 35.2 us (level)
  no operation moved by 1% of the time
where the time goes in v6:
time: 35.2 us; the launch traced here: 35.1 us
  Pallas kernels  34.5 us (98%)
  local copies, waits for them, and re-layouts  0.62 us (2%)
    pallas_call x1, Pallas kernels, shards(): pl.pallas_call(kernel, out_shape=pltpu.VMEM((64, 128), F32), in_specs=[pl...  34.5 us

profile of v6, /device:TPU:1, one launch (start us, length us, event | category | flops | bytes accessed | tf_op | source)
XLA Modules:
  0.0 35.1 jit_solution(16998413462209630667)
XLA Ops:
  0.0 34.5 %shard_map.55 = f32[64,128]{1,0:T(8,128)S(1)} custom-call(bf16[2048,1024]{1,0:T(8,128)(2,1)} %acts.1, bf16[256,8192]{1,0:T(8,128)(2,1)} %cot.1, bf16[16,1024]{1,0:T(8,128)(2,1)} %bitcast.3, bf16[1024,512]{1,0:T(8,128)(2,1)} %proj.1, bf16[128,1024]{1,0:T(8,128)(2,1)} %queries.1), custom_call_target="tpu_custom_call" | custom-call | tf_op jit(solution)/shard_map/pallas_call | solution.py:277
  34.5 0.6 %copy.7 = f32[128,64]{0,1:T(8,128)} copy(f32[128,64]{0,1:T(8,128)S(1)} %bitcast.2) | data formatting | bytes 65536

commit v7 on v6

--- a/solution.py
+++ b/solution.py
@@ -203,11 +203,15 @@
     q_copy.wait()
     both_near, far = pl.ds(0, 32 * NEAR), pl.ds(32 * NEAR, 32 * (16 - NEAR))
     wide[both_near, :] = table[both_near, :].astype(F32)
+
+    pieces = [wide[pl.ds(j, 48, stride=8), :].astype(BF16) for j in range(8)]
+    first = jnp.concatenate(pieces, axis=1)
+    first_cross = nt(first, q_v[...]).astype(BF16)
     take(r_sem.at[3], table.at[far])
     wide[far, :] = table[far, :].astype(F32)
-
-    pieces = [wide[pl.ds(j, 64, stride=8), :].astype(BF16) for j in range(8)]
-    whole = jnp.concatenate(pieces, axis=1)
+    pieces = [wide[pl.ds(384 + j, 16, stride=8), :].astype(BF16) for j in range(8)]
+    rest = jnp.concatenate(pieces, axis=1)
+    whole = jnp.concatenate([first, rest], axis=0)
     gram = nt(whole, jnp.concatenate([whole, whole], axis=0))
     lane = lax.broadcasted_iota(jnp.int32, (32, 128), 1)
     gram = jnp.where(lane < 64, gram[:32], gram[32:])
@@ -215,7 +219,7 @@
     for p in order[:-1]:
         post(send_k, recv_k.at[me], 5, {"tensor": p})
     recv_k[me] = gram
-    cross = nt(whole, q_v[...]).astype(BF16)
+    cross = jnp.concatenate([first_cross, nt(rest, q_v[...]).astype(BF16)], axis=0)
     send_c[...] = cross
     for p in order[:-1]:
         post(send_c, recv_c.at[me], 6, {"tensor": p})

time: 35.2 us -> 35.1 us (level)
  no operation moved by 1% of the time
where the time goes in v7:
time: 35.1 us
  Pallas kernels  34.4 us (98%)
  local copies, waits for them, and re-layouts  0.62 us (2%)
    pallas_call x1, Pallas kernels, shards(): pl.pallas_call(kernel, out_shape=pltpu.VMEM((64, 128), F32), in_specs=[pl...  34.4 us

profile of v7, /device:TPU:1, one launch (start us, length us, event | category | flops | bytes accessed | tf_op | source)
XLA Modules:
  0.0 35.1 jit_solution(7684898316222779715)
XLA Ops:
  0.0 34.4 %shard_map.55 = f32[64,128]{1,0:T(8,128)S(1)} custom-call(bf16[2048,1024]{1,0:T(8,128)(2,1)} %acts.1, bf16[256,8192]{1,0:T(8,128)(2,1)} %cot.1, bf16[16,1024]{1,0:T(8,128)(2,1)} %bitcast.3, bf16[1024,512]{1,0:T(8,128)(2,1)} %proj.1, bf16[128,1024]{1,0:T(8,128)(2,1)} %queries.1), custom_call_target="tpu_custom_call" | custom-call | tf_op jit(solution)/shard_map/pallas_call | solution.py:281
  34.5 0.6 %copy.7 = f32[128,64]{0,1:T(8,128)} copy(f32[128,64]{0,1:T(8,128)S(1)} %bitcast.2) | data formatting | bytes 65536
